TPU v7x, 32 devices: a whole 2x2x4 slice. The times are simulated.
32 devices in a mesh: parts: 2 (over y), attn: 4 (over x, core), ffn: 4 (over z).
Axes of the slice: x: 2, y: 2, z: 4, core: 2. Of those that a mesh axis runs over, the one named last changes fastest.
Arguments:
- query: bfloat16 [4, 64, 16384], P(None, ('parts', 'attn'), 'ffn'), parts along dimension 1
- new_kv: bfloat16 [4, 64, 512], P(None, ('parts', 'attn')), parts along dimension 1
- kv_pool: bfloat16 [2048, 16, 512], P(('parts', 'attn')), parts along dimension 0, may hold values from -6 to 6
- kv_len: int32 [64], P(('parts', 'attn')), parts along dimension 0, may hold values from 1 to 512, as said below
- mig_dest: int32 [32], P('parts'), parts along dimension 0, may hold values from 0 to 3, as said below
- mig_from: int32 [32], P('parts'), parts along dimension 0, may hold values from 0 to 255
- mig_to: int32 [32], P('parts'), parts along dimension 0, may hold values from 0 to 255, as said below
- w_out: bfloat16 [16384, 7168], P('ffn', 'attn'), may hold values from -0.375 to 0.375
- norm_gain: bfloat16 [7168], P('attn'), may hold values from 0.099609375 to 1.8984375
- w_gate: bfloat16 [7168, 18432], P('attn', 'ffn'), may hold values from -0.0625 to 0.0625
- w_up: bfloat16 [7168, 18432], P('attn', 'ffn'), may hold values from -0.0625 to 0.0625
- w_down: bfloat16 [18432, 7168], P('ffn', 'attn'), may hold values from -0.046875 to 0.046875
- resid: bfloat16 [4, 64, 7168], P(None, 'parts', 'attn'), parts along dimension 1
Outputs:
- layer_out: bfloat16 [4, 64, 7168], P(None, ('parts', 'attn'), 'ffn'), parts along dimension 1
There are 2 independent parts, one for each index of `parts`. A program takes and returns all parts, laid end to end along the dimension named above; an argument that names none is the same for every part. Nothing has to cross between parts.
Inputs may be any that keep to these rules, and one draw needn't show every extreme that they name: `kv_len`: some request holds exactly 512 positions in every draw. `mig_dest`: entry j belongs to attention device j // 4 and never names it; a device names 2 distinct destinations, each for exactly 2 of its entries. `mig_to`: no two entries with the same destination name the same destination block.
All inputs are finite; a program needn't handle non-finite values.
Results may differ from a plain program's by a relative error of at most 0.013.
Values may be sent and summed in bfloat16 or wider, within the bound.
A program may use at most 256 MiB of HBM per device.

v0:
```python
import jax
import jax.numpy as jnp
from jax import lax
from jax.sharding import PartitionSpec as P

D = 7168
CAP = 2
STEPS = 4


def stored(value):
    return lax.optimization_barrier(value.astype(jnp.bfloat16)).astype(jnp.float32)


def attend_local(queries, cache_kv, lengths, fresh_kv, head_dim):
    row_count = queries.shape[0]
    per_head = queries.reshape(row_count, -1, head_dim)
    key_part = cache_kv[:, :, :head_dim]
    value_part = cache_kv[:, :, head_dim:]
    score_scale = head_dim ** (-0.5)
    cache_scores = (
        jnp.einsum("rhd,rcd->rhc", per_head, key_part, preferred_element_type=jnp.float32)
        * score_scale
    )
    position = jnp.arange(cache_kv.shape[1], dtype=jnp.int32)
    live_mask = position[None, None, :] < lengths[:, None, None]
    cache_scores = jnp.where(live_mask, cache_scores, -jnp.inf)
    fresh_keys = fresh_kv[:, :, :head_dim]
    fresh_values = fresh_kv[:, :, head_dim:]
    recent_scores = (
        jnp.einsum("rhd,srd->rhs", per_head, fresh_keys, preferred_element_type=jnp.float32)
        * score_scale
    )
    row_max = jnp.maximum(jnp.max(cache_scores, axis=2), jnp.max(recent_scores, axis=2))
    cache_probs = jnp.exp(cache_scores - row_max[:, :, None])
    recent_probs = jnp.exp(recent_scores - row_max[:, :, None])
    weight_sum = jnp.sum(cache_probs, axis=2) + jnp.sum(recent_probs, axis=2)
    weighted = jnp.einsum(
        "rhc,rcd->rhd",
        cache_probs.astype(jnp.bfloat16),
        value_part,
        preferred_element_type=jnp.float32,
    )
    weighted = weighted + jnp.einsum(
        "rhs,srd->rhd",
        recent_probs.astype(jnp.bfloat16),
        fresh_values,
        preferred_element_type=jnp.float32,
    )
    return (weighted / weight_sum[:, :, None]).astype(jnp.bfloat16).reshape(row_count, -1)


def body(
    query,
    new_kv,
    kv_pool,
    kv_len,
    mig_dest,
    mig_from,
    mig_to,
    w_out,
    norm_gain,
    w_gate,
    w_up,
    w_down,
    resid,
):
    peer_count = lax.axis_size("attn")
    my_index = lax.axis_index("attn")
    blocks = kv_pool.shape[0]
    feature_width = kv_pool.shape[2]
    entries = mig_dest.shape[0]
    per_source = entries // peer_count
    entry_index = jnp.arange(entries, dtype=jnp.int32)
    source = entry_index // per_source
    pair_key = source * peer_count + mig_dest
    earlier = (pair_key[:, None] == pair_key[None, :]) & (
        entry_index[None, :] < entry_index[:, None]
    )
    pair_rank = jnp.sum(earlier.astype(jnp.int32), axis=1)
    my_dest = lax.dynamic_slice_in_dim(mig_dest, my_index * per_source, per_source)
    my_from = lax.dynamic_slice_in_dim(mig_from, my_index * per_source, per_source)
    my_rank = lax.dynamic_slice_in_dim(pair_rank, my_index * per_source, per_source)
    send_slot = my_dest * CAP + my_rank
    outgoing = jnp.zeros((peer_count * CAP, kv_pool.shape[1], feature_width), jnp.bfloat16)
    outgoing = (
        outgoing.at[send_slot]
        .set(kv_pool[my_from])
        .reshape(peer_count, CAP, kv_pool.shape[1], feature_width)
    )
    land_slot = jnp.where(mig_dest == my_index, source * CAP + pair_rank, peer_count * CAP)
    landing = (
        jnp.full((peer_count * CAP,), blocks, jnp.int32).at[land_slot].set(mig_to, mode="drop")
    )
    arrived = lax.all_to_all(outgoing, "attn", split_axis=0, concat_axis=0, tiled=True)
    received = arrived.reshape(peer_count * CAP, kv_pool.shape[1], feature_width)
    new_pool = kv_pool.at[landing].set(received, mode="drop")
    cache_kv = new_pool.reshape(kv_len.shape[0], -1, feature_width)
    head_dim = feature_width // 2
    paired = jnp.concatenate([w_gate, w_up], axis=1)
    unit_count = w_gate.shape[1]
    lane_count = lax.axis_size("ffn")
    lane_index = lax.axis_index("ffn")
    outputs = []
    for decode_step in range(STEPS):
        attended = attend_local(
            query[decode_step], cache_kv, kv_len, new_kv[: decode_step + 1], head_dim
        )
        head_part = jnp.dot(
            lax.all_gather(attended, "attn", axis=0, tiled=True),
            w_out,
            preferred_element_type=jnp.float32,
        ).astype(jnp.bfloat16)
        head_sum = lax.psum(head_part.astype(jnp.float32).astype(jnp.bfloat16), "ffn").astype(
            jnp.float32
        )
        state_bf = (resid[decode_step].astype(jnp.float32) + head_sum).astype(jnp.bfloat16)
        widened = state_bf.astype(jnp.float32)
        squares = lax.psum(jnp.sum(widened * widened, axis=1), "attn")
        normed = (
            widened * lax.rsqrt(squares[:, None] / D + 1e-06) * norm_gain.astype(jnp.float32)
        ).astype(jnp.bfloat16)
        gate_up = lax.psum_scatter(
            stored(jnp.dot(normed, paired, preferred_element_type=jnp.float32)).astype(
                jnp.bfloat16
            ),
            "attn",
            scatter_dimension=0,
            tiled=True,
        ).astype(jnp.float32)
        hidden = (jax.nn.silu(gate_up[:, :unit_count]) * gate_up[:, unit_count:]).astype(
            jnp.bfloat16
        )
        unit_part = jnp.dot(
            lax.all_gather(hidden, "attn", axis=0, tiled=True),
            w_down,
            preferred_element_type=jnp.float32,
        ).astype(jnp.bfloat16)
        unit_sum = lax.psum(unit_part.astype(jnp.float32).astype(jnp.bfloat16), "ffn").astype(
            jnp.float32
        )
        layer_out = (widened + unit_sum).astype(jnp.bfloat16)
        by_row = lax.all_to_all(layer_out, "attn", split_axis=0, concat_axis=1, tiled=True)
        share_width = by_row.shape[1] // lane_count
        outputs.append(lax.dynamic_slice_in_dim(by_row, lane_index * share_width, share_width, 1))
    return jnp.stack(outputs)


def solution(mesh):
    placed = (
        P(None, ("parts", "attn"), "ffn"),
        P(None, ("parts", "attn"), None),
        P(("parts", "attn"), None, None),
        P(("parts", "attn")),
        P("parts"),
        P("parts"),
        P("parts"),
        P("ffn", "attn"),
        P("attn"),
        P("attn", "ffn"),
        P("attn", "ffn"),
        P("ffn", "attn"),
        P(None, "parts", "attn"),
    )
    return jax.shard_map(
        body,
        mesh=mesh,
        in_specs=placed,
        out_specs=P(None, ("parts", "attn"), "ffn"),
        check_vma=False,
    )
```

profile of v0, /device:TPU:1, one launch (start us, length us, event | category | flops | bytes accessed | tf_op | source)
XLA Modules:
  0.0 359.9 jit_solution(6377894692168118330)
XLA Ops:
  6.5 4.6 %copy.120 = bf16[256,16,512]{2,1,0:T(8,128)(2,1)} copy(bf16[256,16,512]{2,1,0:T(8,128)(2,1)} %param.15) | data formatting | bytes 8388608
  25.9 13.6 %constant_dynamic-update-slice_fusion.1 = bf16[1792,9216]{1,0:T(8,128)(2,1)} fusion(bf16[1792,4608]{1,0:T(8,128)(2,1)} %param.22), kind=kLoop, calls=%fused_computation.184 | loop fusion | bytes 33030144
  55.0 6.1 %all_gather.24 = bf16[32,4096]{1,0:T(8,128)(2,1)S(1)} all-gather(bf16[8,4096]{1,0:T(8,128)(2,1)S(1)} %bitcast.174), channel_id=1, replica_groups=mesh['parts'=2,'attn'=4,'ffn'=4] {'attn'}, dimensions={0}, use_global_device_ids=true | all-gather | bytes 327680 | tf_op jit(solution)/shard_map/all_gather | solution.py:110
  62.1 6.0 %all_gather.26 = bf16[32,4096]{1,0:T(8,128)(2,1)S(1)} all-gather(bf16[8,4096]{1,0:T(8,128)(2,1)S(1)} %bitcast.175), channel_id=1, replica_groups=mesh['parts'=2,'attn'=4,'ffn'=4] {'attn'}, dimensions={0}, use_global_device_ids=true | all-gather | bytes 327680 | tf_op jit(solution)/shard_map/all_gather | solution.py:110
  68.1 8.5 %convolution_convert_fusion.7 = bf16[32,1792]{1,0:T(8,128)(2,1)} fusion(bf16[32,4096]{1,0:T(8,128)(2,1)S(1)} %all_gather.24, bf16[4096,1792]{1,0:T(8,128)(2,1)} %param.20), kind=kOutput, calls=%fused_computation.11 | convolution fusion | flops 469819392 | bytes 15056896 | tf_op jit(solution)/shard_map/dot_general | solution.py:109
  80.8 5.9 %all_gather.30 = bf16[32,4096]{1,0:T(8,128)(2,1)S(1)} all-gather(bf16[8,4096]{1,0:T(8,128)(2,1)S(1)} %bitcast.176), channel_id=1, replica_groups=mesh['parts'=2,'attn'=4,'ffn'=4] {'attn'}, dimensions={0}, use_global_device_ids=true | all-gather | bytes 327680 | tf_op jit(solution)/shard_map/all_gather | solution.py:110
  90.8 6.0 %all_gather.28 = bf16[32,4096]{1,0:T(8,128)(2,1)S(1)} all-gather(bf16[8,4096]{1,0:T(8,128)(2,1)S(1)} %bitcast.177), channel_id=1, replica_groups=mesh['parts'=2,'attn'=4,'ffn'=4] {'attn'}, dimensions={0}, use_global_device_ids=true | all-gather | bytes 327680 | tf_op jit(solution)/shard_map/all_gather | solution.py:110
  100.1 13.7 %constant_dynamic-update-slice_fusion = bf16[1792,9216]{1,0:T(8,128)(2,1)} fusion(bf16[1792,9216]{1,0:T(8,128)(2,1)} %constant_dynamic-update-slice_fusion.1, bf16[1792,4608]{1,0:T(8,128)(2,1)} %param.23), kind=kLoop, calls=%fused_computation.183 | loop fusion | bytes 33030144 | tf_op jit(solution)/shard_map/concatenate | solution.py:100
  113.8 24.6 %all-reduce.8.cloned.1.call-done = (bf16[32,1792]{1,0:T(8,128)(2,1)}, bf16[32,1792]{1,0:T(8,128)(2,1)}, bf16[32,1792]{1,0:T(8,128)(2,1)}, bf16[32,1792]{1,0:T(8,128)(2,1)}) async-done(((bf16[32,1792]{1,0:T(8,128)(2,1)}, bf16[32,1792]{1,0:T(8,128)(2,1)}, bf16[32,1792]{1,0:T(8,128)(2,1)}, bf16[32,1792]{1,0:T(8,128)(2,1)}), (bf16[32,1792]{1,0:T(8,128)(2,1)}, bf16[32,1792]{1,0:T(8,128)(2,1)}, ...) | async-done | bytes 458768 | tf_op jit(solution)/shard_map/psum | solution.py:114
  139.8 6.8 %all-reduce = (f32[32]{0:T(128)S(1)}, f32[32]{0:T(128)S(1)}, f32[32]{0:T(128)S(1)}, f32[32]{0:T(128)S(1)}) all-reduce(f32[32]{0:T(128)S(1)} %get-tuple-element.7, f32[32]{0:T(128)S(1)} %get-tuple-element.8, f32[32]{0:T(128)S(1)} %get-tuple-element.6, f32[32]{0:T(128)S(1)} %get-tuple-element.5), channel_id=1, replica_groups=mesh['parts'=2,'attn'=4,'ffn'=4] {'attn'}, use_global_device_ids=true, to_apply=%region_35.36 | all-reduce | flops 128 | bytes 1024 | tf_op jit(solution)/shard_map/psum | solution.py:119
  146.6 17.2 %convolution_convert_fusion = bf16[32,9216]{1,0:T(8,128)(2,1)} fusion(bf16[1792,9216]{1,0:T(8,128)(2,1)} %constant_dynamic-update-slice_fusion, f32[32]{0:T(128)S(1)} %add_rsqrt_fusion, f32[1792]{0:T(1024)S(1)} %convert_element_type.236, bf16[32,1792]{1,0:T(8,128)(2,1)} %get-tuple-element.19, bf16[4,32,1792]{2,1,0:T(8,128)(2,1)S(1)} %copy-done.1), kind=kOutput, calls=%fused_computation.4 | convolution fusion | flops 1057718272 | bytes 33858048 | tf_op jit(solution)/shard_map/dot_general | solution.py:124
  163.9 14.6 %convolution_convert_fusion.1 = bf16[32,9216]{1,0:T(8,128)(2,1)} fusion(bf16[1792,9216]{1,0:T(8,128)(2,1)} %constant_dynamic-update-slice_fusion, f32[32]{0:T(128)S(1)} %add_rsqrt_fusion.1, f32[1792]{0:T(1024)S(1)} %convert_element_type.236, bf16[32,1792]{1,0:T(8,128)(2,1)S(1)} %copy-done.5, bf16[4,32,1792]{2,1,0:T(8,128)(2,1)S(1)} %copy-done.1), kind=kOutput, calls=%fused_computation.5 | convolution fusion | flops 1057718272 | bytes 33858048 | tf_op jit(solution)/shard_map/dot_general | solution.py:124
  178.6 14.4 %convolution_convert_fusion.2 = bf16[32,9216]{1,0:T(8,128)(2,1)} fusion(bf16[1792,9216]{1,0:T(8,128)(2,1)} %constant_dynamic-update-slice_fusion, f32[32]{0:T(128)S(1)} %add_rsqrt_fusion.2, f32[1792]{0:T(1024)S(1)} %convert_element_type.236, bf16[32,1792]{1,0:T(8,128)(2,1)S(1)} %copy-done.3, bf16[4,32,1792]{2,1,0:T(8,128)(2,1)S(1)} %copy-done.1), kind=kOutput, calls=%fused_computation.6 | convolution fusion | flops 1057718272 | bytes 33858048 | tf_op jit(solution)/shard_map/dot_general | solution.py:124
  193.4 14.6 %convolution_convert_fusion.3 = bf16[32,9216]{1,0:T(8,128)(2,1)} fusion(bf16[1792,9216]{1,0:T(8,128)(2,1)} %constant_dynamic-update-slice_fusion, f32[1792]{0:T(1024)S(1)} %convert_element_type.236, f32[32]{0:T(128)S(1)} %add_rsqrt_fusion.3, bf16[32,1792]{1,0:T(8,128)(2,1)S(1)} %copy-done.2, bf16[4,32,1792]{2,1,0:T(8,128)(2,1)S(1)} %copy-done.1), kind=kOutput, calls=%fused_computation.7 | convolution fusion | flops 1057718272 | bytes 33858048 | tf_op jit(solution)/shard_map/dot_general | solution.py:124
  209.1 6.3 %all_gather.31 = bf16[32,4608]{1,0:T(8,128)(2,1)S(1)} all-gather(bf16[8,4608]{1,0:T(8,128)(2,1)S(1)} %fusion.128), channel_id=1, replica_groups=mesh['parts'=2,'attn'=4,'ffn'=4] {'attn'}, dimensions={0}, use_global_device_ids=true | all-gather | bytes 368640 | tf_op jit(solution)/shard_map/all_gather | solution.py:135
  216.3 6.0 %all_gather.29 = bf16[32,4608]{1,0:T(8,128)(2,1)S(1)} all-gather(bf16[8,4608]{1,0:T(8,128)(2,1)S(1)} %fusion.129), channel_id=1, replica_groups=mesh['parts'=2,'attn'=4,'ffn'=4] {'attn'}, dimensions={0}, use_global_device_ids=true | all-gather | bytes 368640 | tf_op jit(solution)/shard_map/all_gather | solution.py:135
  222.4 13.0 %reduce-scatter.7.cloned.1.call-done = bf16[8,9216]{1,0:T(8,128)(2,1)} async-done(((bf16[32,9216]{1,0:T(8,128)(2,1)}), bf16[8,9216]{1,0:T(8,128)(2,1)}) %reduce-scatter.7.cloned.1.call-update) | async-done | bytes 147472 | tf_op jit(solution)/shard_map/reduce_scatter | solution.py:123
  236.4 9.4 %convolution_convert_fusion.8 = bf16[32,1792]{1,0:T(8,128)(2,1)} fusion(bf16[32,4608]{1,0:T(8,128)(2,1)S(1)} %all_gather.31, bf16[4608,1792]{1,0:T(8,128)(2,1)} %param.24), kind=kOutput, calls=%fused_computation.12 | convolution fusion | flops 528539648 | bytes 16924672 | tf_op jit(solution)/shard_map/dot_general | solution.py:134
  245.8 9.5 %convolution_convert_fusion.9 = bf16[32,1792]{1,0:T(8,128)(2,1)} fusion(bf16[32,4608]{1,0:T(8,128)(2,1)S(1)} %all_gather.29, bf16[4608,1792]{1,0:T(8,128)(2,1)} %param.24), kind=kOutput, calls=%fused_computation.13 | convolution fusion | flops 528539648 | bytes 16924672 | tf_op jit(solution)/shard_map/dot_general | solution.py:134
  255.3 6.7 %all_gather.27 = bf16[32,4608]{1,0:T(8,128)(2,1)S(1)} all-gather(bf16[8,4608]{1,0:T(8,128)(2,1)S(1)} %fusion.130), channel_id=1, replica_groups=mesh['parts'=2,'attn'=4,'ffn'=4] {'attn'}, dimensions={0}, use_global_device_ids=true | all-gather | bytes 368640 | tf_op jit(solution)/shard_map/all_gather | solution.py:135
  266.6 6.0 %all_gather.25 = bf16[32,4608]{1,0:T(8,128)(2,1)S(1)} all-gather(bf16[8,4608]{1,0:T(8,128)(2,1)S(1)} %fusion.131), channel_id=1, replica_groups=mesh['parts'=2,'attn'=4,'ffn'=4] {'attn'}, dimensions={0}, use_global_device_ids=true | all-gather | bytes 368640 | tf_op jit(solution)/shard_map/all_gather | solution.py:135
  272.7 9.2 %convolution_convert_fusion.11 = bf16[32,1792]{1,0:T(8,128)(2,1)} fusion(bf16[32,4608]{1,0:T(8,128)(2,1)S(1)} %all_gather.25, bf16[4608,1792]{1,0:T(8,128)(2,1)} %param.24), kind=kOutput, calls=%fused_computation.15 | convolution fusion | flops 528539648 | bytes 16924672 | tf_op jit(solution)/shard_map/dot_general | solution.py:134
  281.9 36.7 %all-reduce.6.cloned.1.call-done = (bf16[32,1792]{1,0:T(8,128)(2,1)}, bf16[32,1792]{1,0:T(8,128)(2,1)}, bf16[32,1792]{1,0:T(8,128)(2,1)}, bf16[32,1792]{1,0:T(8,128)(2,1)}) async-done(((bf16[32,1792]{1,0:T(8,128)(2,1)}, bf16[32,1792]{1,0:T(8,128)(2,1)}, bf16[32,1792]{1,0:T(8,128)(2,1)}, bf16[32,1792]{1,0:T(8,128)(2,1)}), (bf16[32,1792]{1,0:T(8,128)(2,1)}, bf16[32,1792]{1,0:T(8,128)(2,1)}, ...) | async-done | bytes 458768 | tf_op jit(solution)/shard_map/psum | solution.py:139
  320.6 5.0 %all-to-all-start.4 = ((bf16[4,8,1792]{2,1,0:T(8,128)(2,1)}), bf16[4,8,1792]{2,1,0:T(8,128)(2,1)S(1)}, u32[]{:S(2)}, u32[]{:S(2)}) async-start(bf16[4,8,1792]{2,1,0:T(8,128)(2,1)} %get-tuple-element.23), calls=%async_computation.8 | async-start | bytes 229376 | tf_op jit(solution)/shard_map/all_to_all | solution.py:143
  (135 shorter events, 81.3 us)
Async XLA Ops:
  18.1 22.9 %all-to-all-start = ((bf16[4,2,16,512]{3,2,1,0:T(8,128)(2,1)}), bf16[4,2,16,512]{3,2,1,0:T(8,128)(2,1)S(1)}, u32[]{:S(2)}, u32[]{:S(2)}) async-start(bf16[4,2,16,512]{3,2,1,0:T(8,128)(2,1)} %bitcast.1), calls=%async_computation | async-start | bytes 262144 | tf_op jit(solution)/shard_map/all_to_all | solution.py:95
  22.3 116.1 %all-reduce.8.cloned.1.call-start = ((), (), s32[]{:S(2)}) async-start(), calls=%async_computation.14 | async-start | bytes 917504 | tf_op jit(solution)/shard_map/psum | solution.py:114
  43.1 18.5 %copy-start = (bf16[256,16,512]{2,1,0:T(8,128)(2,1)S(1)}, bf16[256,16,512]{2,1,0:T(8,128)(2,1)}, u32[]{:S(2)}) copy-start(bf16[256,16,512]{2,1,0:T(8,128)(2,1)} %scatter_fusion.1) | copy-start | bytes 12582916
  50.2 26.4 %slice-start.4 = ((s8[14680064]{0:T(1024)(128)(4,1)}), s8[4194304]{0:T(1024)(128)(4,1)S(1)}, s32[]{:S(2)}) async-start(s8[14680064]{0:T(1024)(128)(4,1)} %bitcast.163), calls=%async_computation.19 | async-start | bytes 8388608
  61.6 15.0 %slice-start.5 = ((s8[14680064]{0:T(1024)(128)(4,1)}), s8[4194304]{0:T(1024)(128)(4,1)S(1)}, s32[]{:S(2)}) async-start(s8[14680064]{0:T(1024)(128)(4,1)} %bitcast.163), calls=%async_computation.20 | async-start | bytes 8388608
  100.1 13.8 %copy-start.7 = (bf16[1792]{0:T(1024)(128)(2,1)S(1)}, bf16[1792]{0:T(1024)(128)(2,1)}, u32[]{:S(2)}) copy-start(bf16[1792]{0:T(1024)(128)(2,1)} %param.21) | copy-start | bytes 10756
  100.1 38.4 %copy-start.1 = (bf16[4,32,1792]{2,1,0:T(8,128)(2,1)S(1)}, bf16[4,32,1792]{2,1,0:T(8,128)(2,1)}, u32[]{:S(2)}) copy-start(bf16[4,32,1792]{2,1,0:T(8,128)(2,1)} %param.25) | copy-start | bytes 1376260
  100.1 108.0 %reduce-scatter.11.cloned.1.call-start = ((), (), s32[]{:S(2)}) async-start(), calls=%async_computation.12 | async-start | bytes 737280 | tf_op jit(solution)/shard_map/reduce_scatter | solution.py:123
  146.6 17.3 %copy-start.5 = (bf16[32,1792]{1,0:T(8,128)(2,1)S(1)}, bf16[32,1792]{1,0:T(8,128)(2,1)}, u32[]{:S(2)}) copy-start(bf16[32,1792]{1,0:T(8,128)(2,1)} %get-tuple-element.20) | copy-start | bytes 344068
  163.8 51.5 %reduce-scatter.9.cloned.1.call-start = ((), (), s32[]{:S(2)}) async-start(), calls=%async_computation.11 | async-start | bytes 737280 | tf_op jit(solution)/shard_map/reduce_scatter | solution.py:123
  163.9 14.7 %copy-start.3 = (bf16[32,1792]{1,0:T(8,128)(2,1)S(1)}, bf16[32,1792]{1,0:T(8,128)(2,1)}, u32[]{:S(2)}) copy-start(bf16[32,1792]{1,0:T(8,128)(2,1)} %get-tuple-element.18) | copy-start | bytes 344068
  178.5 14.8 %copy-start.2 = (bf16[32,1792]{1,0:T(8,128)(2,1)S(1)}, bf16[32,1792]{1,0:T(8,128)(2,1)}, u32[]{:S(2)}) copy-start(bf16[32,1792]{1,0:T(8,128)(2,1)} %get-tuple-element.17) | copy-start | bytes 344068
  178.6 56.8 %reduce-scatter.7.cloned.1.call-start = ((), (), s32[]{:S(2)}) async-start(), calls=%async_computation.10 | async-start | bytes 737280 | tf_op jit(solution)/shard_map/reduce_scatter | solution.py:123
  193.1 72.5 %reduce-scatter.5.cloned.1.call-start = ((), (), s32[]{:S(2)}) async-start(), calls=%async_computation.9 | async-start | bytes 737280 | tf_op jit(solution)/shard_map/reduce_scatter | solution.py:123
  208.0 110.7 %all-reduce.6.cloned.1.call-start = ((), (), s32[]{:S(2)}) async-start(), calls=%async_computation.13 | async-start | bytes 917504 | tf_op jit(solution)/shard_map/psum | solution.py:139
  236.4 25.6 %slice-start = ((s8[16515072]{0:T(1024)(128)(4,1)}), s8[4194304]{0:T(1024)(128)(4,1)S(1)}, s32[]{:S(2)}) async-start(s8[16515072]{0:T(1024)(128)(4,1)} %bitcast.161), calls=%async_computation.15 | async-start | bytes 8388608
  236.4 25.6 %slice-start.1 = ((s8[16515072]{0:T(1024)(128)(4,1)}), s8[4194304]{0:T(1024)(128)(4,1)S(1)}, s32[]{:S(2)}) async-start(s8[16515072]{0:T(1024)(128)(4,1)} %bitcast.161), calls=%async_computation.16 | async-start | bytes 8388608
  245.8 16.2 %slice-start.2 = ((s8[16515072]{0:T(1024)(128)(4,1)}), s8[4194304]{0:T(1024)(128)(4,1)S(1)}, s32[]{:S(2)}) async-start(s8[16515072]{0:T(1024)(128)(4,1)} %bitcast.161), calls=%async_computation.17 | async-start | bytes 8388608
  245.8 16.2 %slice-start.3 = ((s8[16515072]{0:T(1024)(128)(4,1)}), s8[3932160]{0:T(1024)(128)(4,1)S(1)}, s32[]{:S(2)}) async-start(s8[16515072]{0:T(1024)(128)(4,1)} %bitcast.161), calls=%async_computation.18 | async-start | bytes 7864320
  265.6 53.1 %copy-start.4 = (bf16[32,1792]{1,0:T(8,128)(2,1)S(1)}, bf16[32,1792]{1,0:T(8,128)(2,1)}, u32[]{:S(2)}) copy-start(bf16[32,1792]{1,0:T(8,128)(2,1)} %get-tuple-element.19) | copy-start | bytes 344068
  320.6 8.5 %all-to-all-start.4 = ((bf16[4,8,1792]{2,1,0:T(8,128)(2,1)}), bf16[4,8,1792]{2,1,0:T(8,128)(2,1)S(1)}, u32[]{:S(2)}, u32[]{:S(2)}) async-start(bf16[4,8,1792]{2,1,0:T(8,128)(2,1)} %get-tuple-element.23), calls=%async_computation.8 | async-start | bytes 229376 | tf_op jit(solution)/shard_map/all_to_all | solution.py:143
  329.1 7.7 %all-to-all-start.3 = ((bf16[4,8,1792]{2,1,0:T(8,128)(2,1)}), bf16[4,8,1792]{2,1,0:T(8,128)(2,1)S(1)}, u32[]{:S(2)}, u32[]{:S(2)}) async-start(bf16[4,8,1792]{2,1,0:T(8,128)(2,1)} %get-tuple-element.24), calls=%async_computation.6 | async-start | bytes 229376 | tf_op jit(solution)/shard_map/all_to_all | solution.py:143
  336.8 7.7 %all-to-all-start.2 = ((bf16[4,8,1792]{2,1,0:T(8,128)(2,1)}), bf16[4,8,1792]{2,1,0:T(8,128)(2,1)S(1)}, u32[]{:S(2)}, u32[]{:S(2)}) async-start(bf16[4,8,1792]{2,1,0:T(8,128)(2,1)} %get-tuple-element.22), calls=%async_computation.4 | async-start | bytes 229376 | tf_op jit(solution)/shard_map/all_to_all | solution.py:143
  344.6 7.7 %all-to-all-start.1 = ((bf16[4,8,1792]{2,1,0:T(8,128)(2,1)}), bf16[4,8,1792]{2,1,0:T(8,128)(2,1)S(1)}, u32[]{:S(2)}, u32[]{:S(2)}) async-start(bf16[4,8,1792]{2,1,0:T(8,128)(2,1)} %get-tuple-element.21), calls=%async_computation.2 | async-start | bytes 229376 | tf_op jit(solution)/shard_map/all_to_all | solution.py:143
  (4 other events, 44.4 us)
Sparse Core Ops, SparseCore 0:
  100.2 38.2 all-reduce.7
  163.9 21.9 reduce-scatter.10
  188.6 22.0 reduce-scatter.8
  213.3 22.0 reduce-scatter.6
  237.9 22.3 reduce-scatter.4
  282.1 36.5 all-reduce.5
where the time goes:
time: 362 us; the launch traced here: 360 us
  matrix products  125 us (35%)
  waiting for transfers between devices  88.3 us (24%)
  blocking collectives  55.9 us (15%)
  local copies, waits for them, and re-layouts  42.5 us (12%)
  starting transfers between devices  22.5 us (6%)
  between operations  13.9 us (4%)
  other arithmetic  11.9 us (3%)
    dot_general x4, matrix products, body(): jnp.dot(normed, paired, preferred_element_type=jnp.float32)  60.8 us
    psum x1, waiting for transfers between devices, body(): lax.psum(unit_part.astype(jnp.float32).astype(jnp.bfloat16), 'ffn')  36.7 us
    dot_general x4, matrix products, body(): jnp.dot(lax.all_gather(hidden, 'attn', axis=0, tiled=True), w_down, prefe...  31.7 us
    all_gather x4, blocking collectives, body(): lax.all_gather(hidden, 'attn', axis=0, tiled=True)  25.1 us
    psum x1, waiting for transfers between devices, body(): lax.psum(head_part.astype(jnp.float32).astype(jnp.bfloat16), 'ffn')  24.6 us
    all_gather x4, blocking collectives, body(): lax.all_gather(attended, 'attn', axis=0, tiled=True)  24 us
    unnamed x40, local copies, waits for them, and re-layouts  18.4 us
    dot_general x4, matrix products, body(): jnp.dot(lax.all_gather(attended, 'attn', axis=0, tiled=True), w_out, pref...  18.1 us
  transfers between devices with their start and end apart: 11, of which 7 were waited for; matrix products, arithmetic and copies ran while one was open for 28% of the time, Pallas kernels for 0%

commit v1 on v0

--- a/solution.py
+++ b/solution.py
@@ -1,6 +1,8 @@
 import jax
 import jax.numpy as jnp
 from jax import lax
+from jax.experimental import pallas as pl
+from jax.experimental.pallas import tpu as pltpu
 from jax.sharding import PartitionSpec as P
 
 D = 7168
@@ -146,6 +148,544 @@
     return jnp.stack(outputs)
 
 
+MESH = pl.DeviceIdType.MESH
+CHUNKS = 6
+SLOTS = 4
+COLS = 256
+
+
+def near_of(i):
+    return i + 1 - 2 * lax.rem(i, 2)
+
+
+def far_of(i):
+    return lax.rem(i + 2, 4)
+
+
+def layer_kernel(
+    table,
+    sends,
+    lengths,
+    query,
+    new_kv,
+    resid,
+    gain,
+    pool_hbm,
+    w_out,
+    w_gate,
+    w_up,
+    w_down,
+    out,
+    pool,
+    stage,
+    land,
+    cache,
+    q_rows,
+    fresh,
+    att_rows,
+    att,
+    wide,
+    part,
+    zsend,
+    zrecv,
+    state,
+    lhs,
+    sq_send,
+    sq_recv,
+    wbig,
+    wgu,
+    gu_keep,
+    gu_send,
+    gu_recv,
+    gx_send,
+    gx_recv,
+    hid,
+    acc,
+    tsend,
+    lsem,
+    ssem,
+    rsem,
+):
+    a = lax.axis_index("attn")
+    f = lax.axis_index("ffn")
+    p = lax.axis_index("parts")
+    an, af = near_of(a), far_of(a)
+    fn, ff = near_of(f), far_of(f)
+    aff, fff = far_of(an), far_of(fn)
+    blocks = pool_hbm.shape[0]
+    reqs = lengths.shape[0]
+    steps = query.shape[0]
+    rows = steps * reqs
+    hd = pool_hbm.shape[2] // 2
+    heads = query.shape[2] // hd
+    qlen = steps * heads
+    width = w_out.shape[1]
+    units = w_gate.shape[1]
+    cu = units // CHUNKS
+    per_req = blocks // reqs
+    bs = pool_hbm.shape[1]
+
+    def at_attn(i):
+        return (p, i, f)
+
+    def at_ffn(i):
+        return (p, a, i)
+
+    def remote(k, src, dst, dev):
+        return pltpu.make_async_remote_copy(
+            src_ref=src,
+            dst_ref=dst,
+            send_sem=ssem.at[k],
+            recv_sem=rsem.at[k],
+            device_id=dev,
+            device_id_type=MESH,
+        )
+
+    def gu_load(c):
+        s = c % SLOTS
+        return [
+            pltpu.make_async_copy(
+                w.at[:, pl.ds(c * cu, cu)], wgu.at[s, j], lsem.at[2 + s * 2 + j]
+            )
+            for j, w in enumerate((w_gate, w_up))
+        ]
+
+    pool_load = pltpu.make_async_copy(pool_hbm, pool.at[pl.ds(0, blocks)], lsem.at[0])
+    pool_load.start()
+    out_load = pltpu.make_async_copy(w_out, wbig.at[pl.ds(0, w_out.shape[0])], lsem.at[1])
+    out_load.start()
+    for c in range(SLOTS):
+        for d in gu_load(c):
+            d.start()
+
+    barrier = pltpu.get_barrier_semaphore()
+    moved = a != f
+    for o in range(1, 4):
+        pl.semaphore_signal(
+            barrier, inc=1, device_id=at_attn(lax.rem(a + o, 4)), device_id_type=MESH
+        )
+    for peer in (fn, ff):
+        pl.semaphore_signal(barrier, inc=1, device_id=at_ffn(peer), device_id_type=MESH)
+
+    @pl.when(moved)
+    def _():
+        pl.semaphore_signal(barrier, inc=1, device_id=(p, f, a), device_id_type=MESH)
+        pl.semaphore_wait(barrier, 6)
+
+    @pl.when(jnp.logical_not(moved))
+    def _():
+        pl.semaphore_wait(barrier, 5)
+
+    pool_load.wait()
+    mig = []
+    for o in range(1, 4):
+        d = lax.rem(a + o, 4)
+        for s in range(CAP):
+            stage[o - 1, s] = pool[sends[d * CAP + s]]
+        mig.append(
+            remote(o - 1, stage.at[o - 1], land.at[pl.ds(CAP * a, CAP)], at_attn(d))
+        )
+        mig[-1].start()
+
+    for t in range(steps):
+        q_t = query[t].astype(jnp.float32)
+        for h in range(heads):
+            for half in range(2):
+                lo = h * hd + half * 128
+                q_rows[half, pl.ds(t * heads + h, reqs, stride=qlen), :] = q_t[:, lo : lo + 128]
+    fresh[...] = jnp.zeros_like(fresh)
+    for t in range(steps):
+        fresh_t = new_kv[t].astype(jnp.float32)
+        for half in range(4):
+            fresh[half, pl.ds(t, reqs, stride=16), :] = fresh_t[:, half * 128 : (half + 1) * 128]
+    for t in range(steps):
+        wide[t] = resid[t].astype(jnp.float32)
+
+    land[pl.ds(CAP * a, CAP)] = jnp.zeros((CAP, bs, 2 * hd), jnp.bfloat16)
+    for copy in mig:
+        copy.wait()
+    pool[pl.ds(blocks, 4 * CAP)] = land[...]
+
+    scale = hd ** (-0.5)
+
+    def one_request(i, carry):
+        for b in range(per_req):
+            cache[b * bs : (b + 1) * bs, :] = pool[table[i * per_req + b]]
+        mine = pl.ds(i * qlen, qlen)
+        q = jnp.concatenate([q_rows[0, mine, :], q_rows[1, mine, :]], axis=1).astype(jnp.bfloat16)
+        contract = (((1,), (1,)), ((), ()))
+        s1 = (
+            lax.dot_general(q, cache[:, :hd], contract, preferred_element_type=jnp.float32)
+            * scale
+        )
+        pos = lax.broadcasted_iota(jnp.int32, s1.shape, 1)
+        s1 = jnp.where(pos < lengths[i], s1, -jnp.inf)
+        at = pl.ds(i * 16, 16)
+        fk = jnp.concatenate([fresh[0, at, :], fresh[1, at, :]], axis=1).astype(jnp.bfloat16)
+        fv = jnp.concatenate([fresh[2, at, :], fresh[3, at, :]], axis=1).astype(jnp.bfloat16)
+        s2 = lax.dot_general(q, fk, contract, preferred_element_type=jnp.float32) * scale
+        step_of = lax.broadcasted_iota(jnp.int32, s2.shape, 0) // heads
+        s2 = jnp.where(lax.broadcasted_iota(jnp.int32, s2.shape, 1) <= step_of, s2, -jnp.inf)
+        top = jnp.maximum(
+            jnp.max(s1, axis=1, keepdims=True), jnp.max(s2, axis=1, keepdims=True)
+        )
+        p1 = jnp.exp(s1 - top)
+        p2 = jnp.exp(s2 - top)
+        total = jnp.sum(p1, axis=1, keepdims=True) + jnp.sum(p2, axis=1, keepdims=True)
+        o = jnp.dot(
+            p1.astype(jnp.bfloat16), cache[:, hd:], preferred_element_type=jnp.float32
+        ) + jnp.dot(p2.astype(jnp.bfloat16), fv, preferred_element_type=jnp.float32)
+        o = o / total
+        for half in range(2):
+            att_rows[half, pl.ds(i * qlen, qlen), :] = o[:, half * 128 : (half + 1) * 128]
+        return carry
+
+    lax.fori_loop(0, reqs, one_request, 0)
+
+    for h in range(heads):
+        for half in range(2):
+            lo = h * hd + half * 128
+            att[a, :, lo : lo + 128] = jnp.concatenate(
+                [
+                    att_rows[half, pl.ds(t * heads + h, reqs, stride=qlen), :]
+                    for t in range(steps)
+                ],
+                axis=0,
+            ).astype(jnp.bfloat16)
+
+    def gather_begin(k, at, me, near, far, dev):
+        own = [remote(k + 1, at(me), at(me), dev(far)), remote(k, at(me), at(me), dev(near))]
+        for copy in own:
+            copy.start()
+        return own
+
+    def gather_relay(k, own, at, near, far, dev):
+        own[0].wait_recv()
+        relay = remote(k + 2, at(far), at(far), dev(near))
+        relay.start()
+        return own + [relay]
+
+    def gather_end(copies):
+        copies[1].wait_recv()
+        copies[2].wait_recv()
+        for copy in copies:
+            copy.wait_send()
+
+    own = gather_begin(3, lambda i: att.at[i], a, an, af, at_attn)
+    own = gather_relay(3, own, lambda i: att.at[i], an, af, at_attn)
+    out_load.wait()
+    gather_end(own)
+
+    tiles = width // COLS
+    half_tiles = ((tiles + 1) // 2, tiles // 2)
+    col_cuts = ((0, half_tiles[0] * COLS), (half_tiles[0] * COLS, width))
+
+    def out_tile(j, carry):
+        at = pl.ds(pl.multiple_of(j * COLS, COLS), COLS)
+        r = jnp.dot(
+            att[...].reshape(4 * rows, att.shape[2]),
+            wbig[: w_out.shape[0], at],
+            preferred_element_type=jnp.float32,
+        )
+        part[:, :, at] = r.reshape(4, rows, COLS)
+        return carry
+
+    def reduce_near(k, z, lo, hi):
+        zsend[z, 0, :, lo:hi] = part[fff, :, lo:hi].astype(jnp.bfloat16)
+        zsend[z, 1, :, lo:hi] = part[fn, :, lo:hi].astype(jnp.bfloat16)
+        copies = []
+        for j in range(2):
+            piece = (z, j, slice(None), pl.ds(lo, hi - lo))
+            copies.append(remote(k + j, zsend.at[piece], zrecv.at[piece], at_ffn(fn)))
+            copies[-1].start()
+        return copies
+
+    def reduce_far(k, z, lo, hi, copies):
+        copies[0].wait_recv()
+        zsend[z, 2, :, lo:hi] = (
+            part[ff, :, lo:hi] + zrecv[z, 0, :, lo:hi].astype(jnp.float32)
+        ).astype(jnp.bfloat16)
+        piece = (z, 2, slice(None), pl.ds(lo, hi - lo))
+        copy = remote(k + 2, zsend.at[piece], zrecv.at[piece], at_ffn(ff))
+        copy.start()
+        return copies + [copy]
+
+    def reduce_end(z, lo, hi, copies):
+        copies[1].wait_recv()
+        copies[2].wait_recv()
+        total = (
+            part[f, :, lo:hi]
+            + zrecv[z, 1, :, lo:hi].astype(jnp.float32)
+            + zrecv[z, 2, :, lo:hi].astype(jnp.float32)
+        )
+        for copy in copies:
+            copy.wait_send()
+        return total
+
+    def state_at(lo, hi):
+        return lambda i: state.at[i, :, pl.ds(lo, hi - lo)]
+
+    def make_state(lo, hi, total):
+        base = jnp.concatenate(
+            [wide[t, pl.ds(pl.multiple_of(f * reqs, reqs), reqs), lo:hi] for t in range(steps)],
+            axis=0,
+        )
+        state[f, :, lo:hi] = (base + total).astype(jnp.bfloat16)
+
+    (l0, h0), (l1, h1) = col_cuts
+    lax.fori_loop(0, half_tiles[0], out_tile, 0)
+    r0 = reduce_near(6, 0, l0, h0)
+    lax.fori_loop(half_tiles[0], tiles, out_tile, 0)
+    down_load = pltpu.make_async_copy(w_down, wbig, lsem.at[1])
+    down_load.start()
+    r1 = reduce_near(9, 0, l1, h1)
+    r0 = reduce_far(6, 0, l0, h0, r0)
+    r1 = reduce_far(9, 0, l1, h1, r1)
+    make_state(l0, h0, reduce_end(0, l0, h0, r0))
+    g0 = gather_begin(12, state_at(l0, h0), f, fn, ff, at_ffn)
+    make_state(l1, h1, reduce_end(0, l1, h1, r1))
+    g1 = gather_begin(15, state_at(l1, h1), f, fn, ff, at_ffn)
+    g0 = gather_relay(12, g0, state_at(l0, h0), fn, ff, at_ffn)
+    g1 = gather_relay(15, g1, state_at(l1, h1), fn, ff, at_ffn)
+    gather_end(g0)
+    gather_end(g1)
+
+    gain_f = gain[...].astype(jnp.float32)
+
+    def scale_rows(i, carry):
+        w = state[i].astype(jnp.float32)
+        lhs[i] = (w * gain_f).astype(jnp.bfloat16)
+        sq_send[i] = jnp.broadcast_to(jnp.sum(w * w, axis=1, keepdims=True), (rows, 128))
+        return carry
+
+    lax.fori_loop(0, 4, scale_rows, 0)
+    sq = []
+    for o in range(1, 4):
+        d = lax.rem(a + o, 4)
+        sq.append(remote(17 + o, sq_send.at[d], sq_recv.at[a], at_attn(d)))
+        sq[-1].start()
+    sq_recv[a] = sq_send[a]
+
+    K = 21
+    near_copy, far_copy, hid_copy = {}, {}, {}
+
+    def hid_at(c):
+        return lambda i: hid.at[c, i]
+
+    def stage_matmul(c):
+        s = c % SLOTS
+        for d in gu_load(c):
+            d.wait()
+
+        for j in range(2):
+
+            def tile(n, carry):
+                at = pl.ds(pl.multiple_of(n * COLS, COLS), COLS)
+                to = pl.ds(pl.multiple_of(j * cu + n * COLS, COLS), COLS)
+                gu_keep[c % 2, :, :, to] = jnp.dot(
+                    lhs[...].reshape(4 * rows, width),
+                    wgu[s, j, :, at],
+                    preferred_element_type=jnp.float32,
+                ).reshape(4, rows, COLS)
+                return carry
+
+            lax.fori_loop(0, cu // COLS, tile, 0)
+        if c + SLOTS < CHUNKS:
+            for d in gu_load(c + SLOTS):
+                d.start()
+        gu_send[c, 0] = gu_keep[c % 2, aff].astype(jnp.bfloat16)
+        gu_send[c, 1] = gu_keep[c % 2, an].astype(jnp.bfloat16)
+        near_copy[c] = remote(K + c, gu_send.at[c], gu_recv.at[c], at_attn(an))
+        near_copy[c].start()
+
+    def stage_far(c):
+        near_copy[c].wait()
+        gx_send[c] = (gu_keep[c % 2, af] + gu_recv[c, 0].astype(jnp.float32)).astype(
+            jnp.bfloat16
+        )
+        far_copy[c] = remote(K + CHUNKS + c, gx_send.at[c], gx_recv.at[c], at_attn(af))
+        far_copy[c].start()
+        gu_keep[c % 2, a] = gu_keep[c % 2, a] + gu_recv[c, 1].astype(jnp.float32)
+
+    def stage_hidden(c, rs):
+        far_copy[c].wait()
+        gu = gu_keep[c % 2, a] + gx_recv[c].astype(jnp.float32)
+        g = gu[:, :cu] * rs
+        u = gu[:, cu:] * rs
+        hid[c, a] = (g / (1.0 + jnp.exp(-g)) * u).astype(jnp.bfloat16)
+        hid_copy[c] = gather_begin(K + 2 * CHUNKS + 3 * c, hid_at(c), a, an, af, at_attn)
+
+    def stage_relay(c):
+        hid_copy[c] = gather_relay(
+            K + 2 * CHUNKS + 3 * c, hid_copy[c], hid_at(c), an, af, at_attn
+        )
+
+    def stage_down(c):
+        gather_end(hid_copy[c])
+
+        def tile(n, carry):
+            at = pl.ds(pl.multiple_of(n * COLS, COLS), COLS)
+            r = jnp.dot(
+                hid[c].reshape(4 * rows, cu),
+                wbig[c * cu : (c + 1) * cu, at],
+                preferred_element_type=jnp.float32,
+            ).reshape(4, rows, COLS)
+            if c == 0:
+                part[:, :, at] = r
+            else:
+                part[:, :, at] = part[:, :, at] + r
+            return carry
+
+        lax.fori_loop(0, width // COLS, tile, 0)
+
+    stage_matmul(0)
+    stage_far(0)
+    for copy in sq:
+        copy.wait()
+    squares = sq_recv[0] + sq_recv[1] + sq_recv[2] + sq_recv[3]
+    rs = lax.rsqrt(squares[:, :1] / D + 1e-06)
+    stage_matmul(1)
+    stage_far(1)
+    stage_hidden(0, rs)
+    for c in range(2, CHUNKS):
+        stage_matmul(c)
+        stage_far(c)
+        stage_hidden(c - 1, rs)
+        stage_relay(c - 2)
+        if c == 3:
+            down_load.wait()
+        if c >= 3:
+            stage_down(c - 3)
+    stage_relay(CHUNKS - 2)
+    stage_down(CHUNKS - 3)
+    stage_hidden(CHUNKS - 1, rs)
+    stage_down(CHUNKS - 2)
+    stage_relay(CHUNKS - 1)
+    stage_down(CHUNKS - 1)
+
+    K2 = K + 5 * CHUNKS
+    d0 = reduce_near(K2, 1, l0, h0)
+    d1 = reduce_near(K2 + 3, 1, l1, h1)
+    d0 = reduce_far(K2, 1, l0, h0, d0)
+    d1 = reduce_far(K2 + 3, 1, l1, h1, d1)
+    for lo, hi, d in ((l0, h0, d0), (l1, h1, d1)):
+        total = reduce_end(1, lo, hi, d)
+        tsend[:, lo:hi] = (state[f, :, lo:hi].astype(jnp.float32) + total).astype(jnp.bfloat16)
+
+    @pl.when(moved)
+    def _():
+        copy = remote(K2 + 6, tsend, acc, (p, f, a))
+        copy.start()
+        copy.wait()
+
+    @pl.when(jnp.logical_not(moved))
+    def _():
+        acc[...] = tsend[...]
+
+    out[...] = acc[...]
+
+
+def fused_body(
+    query,
+    new_kv,
+    kv_pool,
+    kv_len,
+    mig_dest,
+    mig_from,
+    mig_to,
+    w_out,
+    norm_gain,
+    w_gate,
+    w_up,
+    w_down,
+    resid,
+):
+    a = lax.axis_index("attn")
+    blocks, bs, kvw = kv_pool.shape
+    steps, reqs, qw = query.shape
+    rows = steps * reqs
+    width = w_out.shape[1]
+    units = w_gate.shape[1]
+    cu = units // CHUNKS
+    qlen = steps * (qw // (kvw // 2))
+    entries = mig_dest.shape[0]
+    e = jnp.arange(entries, dtype=jnp.int32)
+    source = e // (entries // 4)
+    key = source * 4 + mig_dest
+    earlier = (key[:, None] == key[None, :]) & (e[None, :] < e[:, None])
+    rank = jnp.sum(earlier.astype(jnp.int32), axis=1)
+    slot = jnp.arange(4 * CAP, dtype=jnp.int32)
+    picked = (source == a)[None, :] & ((mig_dest * CAP + rank)[None, :] == slot[:, None])
+    sends = jnp.sum(jnp.where(picked, mig_from[None, :], 0), axis=1).astype(jnp.int32)
+    block = jnp.arange(blocks, dtype=jnp.int32)
+    lands = (mig_dest == a)[None, :] & (mig_to[None, :] == block[:, None])
+    table = jnp.maximum(
+        block,
+        jnp.max(jnp.where(lands, (blocks + source * CAP + rank)[None, :], 0), axis=1),
+    ).astype(jnp.int32)
+
+    bf, f32 = jnp.bfloat16, jnp.float32
+    smem = pl.BlockSpec(memory_space=pltpu.SMEM)
+    vmem = pl.BlockSpec(memory_space=pltpu.VMEM)
+    anym = pl.BlockSpec(memory_space=pl.ANY)
+    copies = 21 + 5 * CHUNKS + 7
+    big = max(w_out.shape[0], w_down.shape[0])
+    result = pl.pallas_call(
+        layer_kernel,
+        out_shape=jax.ShapeDtypeStruct((rows, width), bf),
+        in_specs=[smem] * 3 + [vmem] * 4 + [anym] * 5,
+        out_specs=vmem,
+        scratch_shapes=[
+            pltpu.VMEM((blocks + 4 * CAP, bs, kvw), bf),
+            pltpu.VMEM((3, CAP, bs, kvw), bf),
+            pltpu.VMEM((4 * CAP, bs, kvw), bf),
+            pltpu.VMEM((blocks // reqs * bs, kvw), bf),
+            pltpu.VMEM((2, reqs * qlen, 128), f32),
+            pltpu.VMEM((4, reqs * 16, 128), f32),
+            pltpu.VMEM((2, reqs * qlen, 128), f32),
+            pltpu.VMEM((4, rows, qw), bf),
+            pltpu.VMEM((steps, 4 * reqs, width), f32),
+            pltpu.VMEM((4, rows, width), f32),
+            pltpu.VMEM((2, 3, rows, width), bf),
+            pltpu.VMEM((2, 3, rows, width), bf),
+            pltpu.VMEM((4, rows, width), bf),
+            pltpu.VMEM((4, rows, width), bf),
+            pltpu.VMEM((4, rows, 128), f32),
+            pltpu.VMEM((4, rows, 128), f32),
+            pltpu.VMEM((big, width), bf),
+            pltpu.VMEM((SLOTS, 2, w_gate.shape[0], cu), bf),
+            pltpu.VMEM((2, 4, rows, 2 * cu), f32),
+            pltpu.VMEM((CHUNKS, 2, rows, 2 * cu), bf),
+            pltpu.VMEM((CHUNKS, 2, rows, 2 * cu), bf),
+            pltpu.VMEM((CHUNKS, rows, 2 * cu), bf),
+            pltpu.VMEM((CHUNKS, rows, 2 * cu), bf),
+            pltpu.VMEM((CHUNKS, 4, rows, cu), bf),
+            pltpu.VMEM((rows, width), bf),
+            pltpu.VMEM((rows, width), bf),
+            pltpu.SemaphoreType.DMA((2 + 2 * SLOTS,)),
+            pltpu.SemaphoreType.DMA((copies,)),
+            pltpu.SemaphoreType.DMA((copies,)),
+        ],
+        compiler_params=pltpu.CompilerParams(
+            collective_id=0, has_side_effects=True, vmem_limit_bytes=60 * 1024 * 1024
+        ),
+    )(
+        table,
+        sends,
+        kv_len,
+        query,
+        new_kv,
+        resid,
+        norm_gain.reshape(1, -1),
+        kv_pool,
+        w_out,
+        w_gate,
+        w_up,
+        w_down,
+    )
+    return result.reshape(steps, reqs, width)
+
+
 def solution(mesh):
     placed = (
         P(None, ("parts", "attn"), "ffn"),
@@ -162,8 +702,9 @@
         P("ffn", "attn"),
         P(None, "parts", "attn"),
     )
+    use_kernel = mesh.shape["attn"] == 4 and mesh.shape["ffn"] == 4
     return jax.shard_map(
-        body,
+        fused_body if use_kernel else body,
         mesh=mesh,
         in_specs=placed,
         out_specs=P(None, ("parts", "attn"), "ffn"),

time: 362 us -> 107 us (0.30)
  matrix products: 125 us -> 0 us
  Pallas kernels: 0 us -> 98 us
  waiting for transfers between devices: 88.3 us -> 0 us
  blocking collectives: 55.9 us -> 0 us
  local copies, waits for them, and re-layouts: 42.5 us -> 2.84 us
  starting transfers between devices: 22.5 us -> 0 us
  between operations: 13.9 us -> 0.01 us
  other arithmetic: 11.9 us -> 4.78 us
    dot_general x27 -> x0, matrix products: 125 us -> none  [the longest x4 60.8 us: body(): jnp.dot(normed, paired, preferred_element_type=jnp.float32)]
    pallas_call x0 -> x1, Pallas kernels: none -> 98 us  [fused_body(): pl.pallas_call(layer_kernel, out_shape=jax.ShapeDtypeStruct((rows, width)...]
    psum x2 -> x0, waiting for transfers between devices: 61.4 us -> none  [the longest x1 36.7 us: body(): lax.psum(unit_part.astype(jnp.float32).astype(jnp.bfloat16), 'ffn')]
    all_gather x8 -> x0, blocking collectives: 49.2 us -> none  [the longest x4 25.1 us: body(): lax.all_gather(hidden, 'attn', axis=0, tiled=True)]
    all_to_all x5 -> x0, starting transfers between devices: 22.1 us -> none  [the longest x4 17.9 us: body(): lax.all_to_all(layer_out, 'attn', split_axis=0, concat_axis=1, tiled=True)]
    unnamed x40 -> x1, local copies, waits for them, and re-layouts: 18.4 us -> 1.55 us
    all_to_all x5 -> x0, waiting for transfers between devices: 13.9 us -> none  [the longest x4 13.9 us: body(): lax.all_to_all(layer_out, 'attn', split_axis=0, concat_axis=1, tiled=True)]
    concatenate x1 -> x0, local copies, waits for them, and re-layouts: 13.7 us -> none  [body(): paired = jnp.concatenate([w_gate, w_up], axis=1)]
  transfers between devices with their start and end apart: 11 -> 0, of which waited for: 7 -> 0; matrix products, arithmetic and copies ran while one was open for 28% -> 0% of each run, Pallas kernels for 0% -> 0%
where the time goes in v1:
time: 107 us; the launch traced here: 106 us
  Pallas kernels  98 us (92%)
  other arithmetic  4.78 us (4%)
  local copies, waits for them, and re-layouts  2.84 us (3%)
    pallas_call x1, Pallas kernels, fused_body(): pl.pallas_call(layer_kernel, out_shape=jax.ShapeDtypeStruct((rows, width)...  98 us

profile of v1, /device:TPU:1, one launch (start us, length us, event | category | flops | bytes accessed | tf_op | source)
XLA Modules:
  0.0 105.6 jit_solution(11246673967805578517)
XLA Ops:
  0.0 0.7 multiply_add_fusion.1
  0.7 0.2 convert_reduce_fusion
  0.8 0.7 multiply_add_fusion
  1.5 0.7 fusion.3
  2.2 1.3 %select_reduce_fusion.1.sends = s32[8]{0:T(128)} fusion(s32[16]{0:T(128)} %param.18, s32[16]{0:T(128)S(1)} %get-tuple-element.5, pred[16]{0:T(512)(128)(4,1)S(1)} %get-tuple-element.7), kind=kLoop, calls=%fused_computation.6 | loop fusion | flops 504 | bytes 176 | tf_op jit(solution)/shard_map/reduce_sum | solution.py:619
  3.4 0.7 select_reduce_fusion
  4.2 0.6 iota_maximum_fusion.table
  4.8 1.3 %reshape.33.gain = bf16[1,1792]{1,0:T(2,128)(2,1)} reshape(bf16[1792]{0:T(1024)(128)(2,1)} %param.21) | data formatting | bytes 7168 | tf_op jit(solution)/shard_map/reshape | solution.py:679
  6.1 98.0 %shard_map.127 = bf16[32,1792]{1,0:T(8,128)(2,1)} custom-call(s32[256]{0:T(256)} %iota_maximum_fusion.table, s32[8]{0:T(128)} %select_reduce_fusion.1.sends, s32[8]{0:T(128)} %lengths.1, bf16[4,8,4096]{2,1,0:T(8,128)(2,1)} %query.1, bf16[4,8,512]{2,1,0:T(8,128)(2,1)} %new_kv.1, bf16[4,32,1792]{2,1,0:T(8,128)(2,1)} %resid.1, bf16[1,1792]{1,0:T(2,128)(2,1)} %reshape.33.gain, ...), custom_call_target="tpu_custom_call" | custom-call | tf_op jit(solution)/shard_map/pallas_call | solution.py:633
  104.1 1.6 %copy.15 = bf16[4,8,1792]{2,1,0:T(8,128)(2,1)} copy(bf16[4,8,1792]{2,1,0:T(8,128)(2,1)} %bitcast.1) | data formatting | bytes 229376

commit v2 on v1

--- a/solution.py
+++ b/solution.py
@@ -151,6 +151,8 @@
 MESH = pl.DeviceIdType.MESH
 CHUNKS = 6
 SLOTS = 4
+PAIR = 2
+KEEP = 3
 COLS = 256
 
 
@@ -163,8 +165,9 @@
 
 
 def layer_kernel(
-    table,
-    sends,
+    mig_dest,
+    mig_from,
+    mig_to,
     lengths,
     query,
     new_kv,
@@ -253,10 +256,6 @@
     pool_load = pltpu.make_async_copy(pool_hbm, pool.at[pl.ds(0, blocks)], lsem.at[0])
     pool_load.start()
     out_load = pltpu.make_async_copy(w_out, wbig.at[pl.ds(0, w_out.shape[0])], lsem.at[1])
-    out_load.start()
-    for c in range(SLOTS):
-        for d in gu_load(c):
-            d.start()
 
     barrier = pltpu.get_barrier_semaphore()
     moved = a != f
@@ -276,16 +275,32 @@
     def _():
         pl.semaphore_wait(barrier, 5)
 
+    per_source = mig_dest.shape[0] // 4
+
+    def entry_of(source, dest, rank, values, none):
+        seen = jnp.int32(0)
+        found = jnp.int32(none)
+        for e in range(per_source):
+            here = mig_dest[source * per_source + e] == dest
+            hit = jnp.logical_and(here, seen == rank)
+            found = jnp.where(hit, values[source * per_source + e], found)
+            seen = seen + jnp.where(here, 1, 0)
+        return found
+
     pool_load.wait()
     mig = []
     for o in range(1, 4):
         d = lax.rem(a + o, 4)
         for s in range(CAP):
-            stage[o - 1, s] = pool[sends[d * CAP + s]]
+            stage[o - 1, s] = pool[entry_of(a, d, s, mig_from, 0)]
         mig.append(
             remote(o - 1, stage.at[o - 1], land.at[pl.ds(CAP * a, CAP)], at_attn(d))
         )
         mig[-1].start()
+    out_load.start()
+    for c in range(SLOTS):
+        for d in gu_load(c):
+            d.start()
 
     for t in range(steps):
         q_t = query[t].astype(jnp.float32)
@@ -306,24 +321,34 @@
         copy.wait()
     pool[pl.ds(blocks, 4 * CAP)] = land[...]
 
+    landed = []
+    for o in range(1, 4):
+        source = lax.rem(a + o, 4)
+        for s in range(CAP):
+            landed.append((entry_of(source, a, s, mig_to, -1), blocks + CAP * source + s))
+
     scale = hd ** (-0.5)
 
-    def one_request(i, carry):
+    contract = (((1,), (1,)), ((), ()))
+
+    def score(i, u):
         for b in range(per_req):
-            cache[b * bs : (b + 1) * bs, :] = pool[table[i * per_req + b]]
+            block = i * per_req + b
+            index = block
+            for to, slot in landed:
+                index = jnp.where(to == block, slot, index)
+            cache[u, b * bs : (b + 1) * bs, :] = pool[index]
         mine = pl.ds(i * qlen, qlen)
         q = jnp.concatenate([q_rows[0, mine, :], q_rows[1, mine, :]], axis=1).astype(jnp.bfloat16)
-        contract = (((1,), (1,)), ((), ()))
-        s1 = (
-            lax.dot_general(q, cache[:, :hd], contract, preferred_element_type=jnp.float32)
-            * scale
-        )
+        s1 = lax.dot_general(q, cache[u, :, :hd], contract, preferred_element_type=jnp.float32)
+        at = pl.ds(i * 16, 16)
+        fk = jnp.concatenate([fresh[0, at, :], fresh[1, at, :]], axis=1).astype(jnp.bfloat16)
+        s2 = lax.dot_general(q, fk, contract, preferred_element_type=jnp.float32)
+        return s1 * scale, s2 * scale
+
+    def softmax(i, s1, s2):
         pos = lax.broadcasted_iota(jnp.int32, s1.shape, 1)
         s1 = jnp.where(pos < lengths[i], s1, -jnp.inf)
-        at = pl.ds(i * 16, 16)
-        fk = jnp.concatenate([fresh[0, at, :], fresh[1, at, :]], axis=1).astype(jnp.bfloat16)
-        fv = jnp.concatenate([fresh[2, at, :], fresh[3, at, :]], axis=1).astype(jnp.bfloat16)
-        s2 = lax.dot_general(q, fk, contract, preferred_element_type=jnp.float32) * scale
         step_of = lax.broadcasted_iota(jnp.int32, s2.shape, 0) // heads
         s2 = jnp.where(lax.broadcasted_iota(jnp.int32, s2.shape, 1) <= step_of, s2, -jnp.inf)
         top = jnp.maximum(
@@ -332,26 +357,41 @@
         p1 = jnp.exp(s1 - top)
         p2 = jnp.exp(s2 - top)
         total = jnp.sum(p1, axis=1, keepdims=True) + jnp.sum(p2, axis=1, keepdims=True)
-        o = jnp.dot(
-            p1.astype(jnp.bfloat16), cache[:, hd:], preferred_element_type=jnp.float32
-        ) + jnp.dot(p2.astype(jnp.bfloat16), fv, preferred_element_type=jnp.float32)
-        o = o / total
-        for half in range(2):
-            att_rows[half, pl.ds(i * qlen, qlen), :] = o[:, half * 128 : (half + 1) * 128]
+        return p1.astype(jnp.bfloat16), p2.astype(jnp.bfloat16), total
+
+    def attend(i, u, p1, p2, total):
+        at = pl.ds(i * 16, 16)
+        fv = jnp.concatenate([fresh[2, at, :], fresh[3, at, :]], axis=1).astype(jnp.bfloat16)
+        o = jnp.dot(p1, cache[u, :, hd:], preferred_element_type=jnp.float32) + jnp.dot(
+            p2, fv, preferred_element_type=jnp.float32
+        )
+        return o / total
+
+    def request_pair(k, carry):
+        first = k * PAIR
+        scored = [score(first + u, u) for u in range(PAIR)]
+        probs = [softmax(first + u, *scored[u]) for u in range(PAIR)]
+        outs = [attend(first + u, u, *probs[u]) for u in range(PAIR)]
+        for u in range(PAIR):
+            for half in range(2):
+                att_rows[half, pl.ds((first + u) * qlen, qlen), :] = outs[u][
+                    :, half * 128 : (half + 1) * 128
+                ]
         return carry
 
-    lax.fori_loop(0, reqs, one_request, 0)
-
-    for h in range(heads):
-        for half in range(2):
-            lo = h * hd + half * 128
-            att[a, :, lo : lo + 128] = jnp.concatenate(
-                [
-                    att_rows[half, pl.ds(t * heads + h, reqs, stride=qlen), :]
-                    for t in range(steps)
-                ],
-                axis=0,
-            ).astype(jnp.bfloat16)
+    lax.fori_loop(0, reqs // PAIR, request_pair, 0)
+
+    def lay_out(first, last):
+        for h in range(first, last):
+            for half in range(2):
+                lo = h * hd + half * 128
+                att[a, :, lo : lo + 128] = jnp.concatenate(
+                    [
+                        att_rows[half, pl.ds(t * heads + h, reqs, stride=qlen), :]
+                        for t in range(steps)
+                    ],
+                    axis=0,
+                ).astype(jnp.bfloat16)
 
     def gather_begin(k, at, me, near, far, dev):
         own = [remote(k + 1, at(me), at(me), dev(far)), remote(k, at(me), at(me), dev(near))]
@@ -371,10 +411,18 @@
         for copy in copies:
             copy.wait_send()
 
-    own = gather_begin(3, lambda i: att.at[i], a, an, af, at_attn)
-    own = gather_relay(3, own, lambda i: att.at[i], an, af, at_attn)
+    kh = heads // 2 * hd
+
+    def att_at(part_index):
+        return lambda i: att.at[i, :, pl.ds(part_index * kh, kh)]
+
+    lay_out(0, heads // 2)
+    a0 = gather_begin(3, att_at(0), a, an, af, at_attn)
+    lay_out(heads // 2, heads)
+    a1 = gather_begin(18 + 3, att_at(1), a, an, af, at_attn)
+    a0 = gather_relay(3, a0, att_at(0), an, af, at_attn)
     out_load.wait()
-    gather_end(own)
+    gather_end(a0)
 
     tiles = width // COLS
     half_tiles = ((tiles + 1) // 2, tiles // 2)
@@ -383,11 +431,21 @@
     def out_tile(j, carry):
         at = pl.ds(pl.multiple_of(j * COLS, COLS), COLS)
         r = jnp.dot(
-            att[...].reshape(4 * rows, att.shape[2]),
-            wbig[: w_out.shape[0], at],
+            att[:, :, :kh].reshape(4 * rows, kh),
+            wbig[:kh, at],
             preferred_element_type=jnp.float32,
         )
         part[:, :, at] = r.reshape(4, rows, COLS)
+        return carry
+
+    def out_tile_rest(j, carry):
+        at = pl.ds(pl.multiple_of(j * COLS, COLS), COLS)
+        r = jnp.dot(
+            att[:, :, kh:].reshape(4 * rows, kh),
+            wbig[kh : 2 * kh, at],
+            preferred_element_type=jnp.float32,
+        )
+        part[:, :, at] = part[:, :, at] + r.reshape(4, rows, COLS)
         return carry
 
     def reduce_near(k, z, lo, hi):
@@ -434,8 +492,12 @@
 
     (l0, h0), (l1, h1) = col_cuts
     lax.fori_loop(0, half_tiles[0], out_tile, 0)
+    a1 = gather_relay(18 + 3, a1, att_at(1), an, af, at_attn)
+    lax.fori_loop(half_tiles[0], tiles, out_tile, 0)
+    gather_end(a1)
+    lax.fori_loop(0, half_tiles[0], out_tile_rest, 0)
     r0 = reduce_near(6, 0, l0, h0)
-    lax.fori_loop(half_tiles[0], tiles, out_tile, 0)
+    lax.fori_loop(half_tiles[0], tiles, out_tile_rest, 0)
     down_load = pltpu.make_async_copy(w_down, wbig, lsem.at[1])
     down_load.start()
     r1 = reduce_near(9, 0, l1, h1)
@@ -450,7 +512,7 @@
     gather_end(g0)
     gather_end(g1)
 
-    gain_f = gain[...].astype(jnp.float32)
+    gain_f = gain[...].astype(jnp.float32).reshape(1, width)
 
     def scale_rows(i, carry):
         w = state[i].astype(jnp.float32)
@@ -466,7 +528,7 @@
         sq[-1].start()
     sq_recv[a] = sq_send[a]
 
-    K = 21
+    K = 24
     near_copy, far_copy, hid_copy = {}, {}, {}
 
     def hid_at(c):
@@ -482,7 +544,7 @@
             def tile(n, carry):
                 at = pl.ds(pl.multiple_of(n * COLS, COLS), COLS)
                 to = pl.ds(pl.multiple_of(j * cu + n * COLS, COLS), COLS)
-                gu_keep[c % 2, :, :, to] = jnp.dot(
+                gu_keep[c % KEEP, :, :, to] = jnp.dot(
                     lhs[...].reshape(4 * rows, width),
                     wgu[s, j, :, at],
                     preferred_element_type=jnp.float32,
@@ -493,23 +555,23 @@
         if c + SLOTS < CHUNKS:
             for d in gu_load(c + SLOTS):
                 d.start()
-        gu_send[c, 0] = gu_keep[c % 2, aff].astype(jnp.bfloat16)
-        gu_send[c, 1] = gu_keep[c % 2, an].astype(jnp.bfloat16)
+        gu_send[c, 0] = gu_keep[c % KEEP, aff].astype(jnp.bfloat16)
+        gu_send[c, 1] = gu_keep[c % KEEP, an].astype(jnp.bfloat16)
         near_copy[c] = remote(K + c, gu_send.at[c], gu_recv.at[c], at_attn(an))
         near_copy[c].start()
 
     def stage_far(c):
         near_copy[c].wait()
-        gx_send[c] = (gu_keep[c % 2, af] + gu_recv[c, 0].astype(jnp.float32)).astype(
+        gx_send[c] = (gu_keep[c % KEEP, af] + gu_recv[c, 0].astype(jnp.float32)).astype(
             jnp.bfloat16
         )
         far_copy[c] = remote(K + CHUNKS + c, gx_send.at[c], gx_recv.at[c], at_attn(af))
         far_copy[c].start()
-        gu_keep[c % 2, a] = gu_keep[c % 2, a] + gu_recv[c, 1].astype(jnp.float32)
+        gu_keep[c % KEEP, a] = gu_keep[c % KEEP, a] + gu_recv[c, 1].astype(jnp.float32)
 
     def stage_hidden(c, rs):
         far_copy[c].wait()
-        gu = gu_keep[c % 2, a] + gx_recv[c].astype(jnp.float32)
+        gu = gu_keep[c % KEEP, a] + gx_recv[c].astype(jnp.float32)
         g = gu[:, :cu] * rs
         u = gu[:, cu:] * rs
         hid[c, a] = (g / (1.0 + jnp.exp(-g)) * u).astype(jnp.bfloat16)
@@ -520,8 +582,9 @@
             K + 2 * CHUNKS + 3 * c, hid_copy[c], hid_at(c), an, af, at_attn
         )
 
-    def stage_down(c):
-        gather_end(hid_copy[c])
+    def stage_down(c, first, last):
+        if first == 0:
+            gather_end(hid_copy[c])
 
         def tile(n, carry):
             at = pl.ds(pl.multiple_of(n * COLS, COLS), COLS)
@@ -536,53 +599,56 @@
                 part[:, :, at] = part[:, :, at] + r
             return carry
 
-        lax.fori_loop(0, width // COLS, tile, 0)
+        lax.fori_loop(first, last, tile, 0)
 
     stage_matmul(0)
-    stage_far(0)
     for copy in sq:
         copy.wait()
     squares = sq_recv[0] + sq_recv[1] + sq_recv[2] + sq_recv[3]
     rs = lax.rsqrt(squares[:, :1] / D + 1e-06)
-    stage_matmul(1)
-    stage_far(1)
-    stage_hidden(0, rs)
-    for c in range(2, CHUNKS):
-        stage_matmul(c)
-        stage_far(c)
-        stage_hidden(c - 1, rs)
-        stage_relay(c - 2)
-        if c == 3:
+    for c in range(1, CHUNKS + 4):
+        if c < CHUNKS:
+            stage_matmul(c)
+        if c - 1 < CHUNKS:
+            stage_far(c - 1)
+        if 0 <= c - 2 < CHUNKS:
+            stage_hidden(c - 2, rs)
+        if 0 <= c - 3 < CHUNKS:
+            stage_relay(c - 3)
+        if c == 4:
             down_load.wait()
-        if c >= 3:
-            stage_down(c - 3)
-    stage_relay(CHUNKS - 2)
-    stage_down(CHUNKS - 3)
-    stage_hidden(CHUNKS - 1, rs)
-    stage_down(CHUNKS - 2)
-    stage_relay(CHUNKS - 1)
-    stage_down(CHUNKS - 1)
+        if 0 <= c - 4 < CHUNKS - 1:
+            stage_down(c - 4, 0, tiles)
 
     K2 = K + 5 * CHUNKS
+    stage_down(CHUNKS - 1, 0, half_tiles[0])
     d0 = reduce_near(K2, 1, l0, h0)
+    stage_down(CHUNKS - 1, half_tiles[0], tiles)
     d1 = reduce_near(K2 + 3, 1, l1, h1)
     d0 = reduce_far(K2, 1, l0, h0, d0)
     d1 = reduce_far(K2 + 3, 1, l1, h1, d1)
-    for lo, hi, d in ((l0, h0, d0), (l1, h1, d1)):
+    def turn(k, lo, hi):
+        at = (slice(None), pl.ds(lo, hi - lo))
+        return remote(k, tsend.at[at], acc.at[at], (p, f, a))
+
+    for k, lo, hi, d in ((K2 + 6, l0, h0, d0), (K2 + 7, l1, h1, d1)):
         total = reduce_end(1, lo, hi, d)
         tsend[:, lo:hi] = (state[f, :, lo:hi].astype(jnp.float32) + total).astype(jnp.bfloat16)
 
+        @pl.when(moved)
+        def _():
+            turn(k, lo, hi).start()
+
     @pl.when(moved)
     def _():
-        copy = remote(K2 + 6, tsend, acc, (p, f, a))
-        copy.start()
-        copy.wait()
+        turn(K2 + 6, l0, h0).wait()
+        turn(K2 + 7, l1, h1).wait()
 
     @pl.when(jnp.logical_not(moved))
     def _():
         acc[...] = tsend[...]
 
-    out[...] = acc[...]
+    out[...] = acc[...].astype(jnp.float32).reshape(steps, reqs, width).astype(jnp.bfloat16)
 
 
 def fused_body(
@@ -600,7 +666,6 @@
     w_down,
     resid,
 ):
-    a = lax.axis_index("attn")
     blocks, bs, kvw = kv_pool.shape
     steps, reqs, qw = query.shape
     rows = steps * reqs
@@ -608,38 +673,22 @@
     units = w_gate.shape[1]
     cu = units // CHUNKS
     qlen = steps * (qw // (kvw // 2))
-    entries = mig_dest.shape[0]
-    e = jnp.arange(entries, dtype=jnp.int32)
-    source = e // (entries // 4)
-    key = source * 4 + mig_dest
-    earlier = (key[:, None] == key[None, :]) & (e[None, :] < e[:, None])
-    rank = jnp.sum(earlier.astype(jnp.int32), axis=1)
-    slot = jnp.arange(4 * CAP, dtype=jnp.int32)
-    picked = (source == a)[None, :] & ((mig_dest * CAP + rank)[None, :] == slot[:, None])
-    sends = jnp.sum(jnp.where(picked, mig_from[None, :], 0), axis=1).astype(jnp.int32)
-    block = jnp.arange(blocks, dtype=jnp.int32)
-    lands = (mig_dest == a)[None, :] & (mig_to[None, :] == block[:, None])
-    table = jnp.maximum(
-        block,
-        jnp.max(jnp.where(lands, (blocks + source * CAP + rank)[None, :], 0), axis=1),
-    ).astype(jnp.int32)
-
     bf, f32 = jnp.bfloat16, jnp.float32
     smem = pl.BlockSpec(memory_space=pltpu.SMEM)
     vmem = pl.BlockSpec(memory_space=pltpu.VMEM)
     anym = pl.BlockSpec(memory_space=pl.ANY)
-    copies = 21 + 5 * CHUNKS + 7
+    copies = 24 + 5 * CHUNKS + 8
     big = max(w_out.shape[0], w_down.shape[0])
     result = pl.pallas_call(
         layer_kernel,
-        out_shape=jax.ShapeDtypeStruct((rows, width), bf),
-        in_specs=[smem] * 3 + [vmem] * 4 + [anym] * 5,
+        out_shape=jax.ShapeDtypeStruct((steps, reqs, width), bf),
+        in_specs=[smem] * 4 + [vmem] * 4 + [anym] * 5,
         out_specs=vmem,
         scratch_shapes=[
             pltpu.VMEM((blocks + 4 * CAP, bs, kvw), bf),
             pltpu.VMEM((3, CAP, bs, kvw), bf),
             pltpu.VMEM((4 * CAP, bs, kvw), bf),
-            pltpu.VMEM((blocks // reqs * bs, kvw), bf),
+            pltpu.VMEM((PAIR, blocks // reqs * bs, kvw), bf),
             pltpu.VMEM((2, reqs * qlen, 128), f32),
             pltpu.VMEM((4, reqs * 16, 128), f32),
             pltpu.VMEM((2, reqs * qlen, 128), f32),
@@ -654,7 +703,7 @@
             pltpu.VMEM((4, rows, 128), f32),
             pltpu.VMEM((big, width), bf),
             pltpu.VMEM((SLOTS, 2, w_gate.shape[0], cu), bf),
-            pltpu.VMEM((2, 4, rows, 2 * cu), f32),
+            pltpu.VMEM((KEEP, 4, rows, 2 * cu), f32),
             pltpu.VMEM((CHUNKS, 2, rows, 2 * cu), bf),
             pltpu.VMEM((CHUNKS, 2, rows, 2 * cu), bf),
             pltpu.VMEM((CHUNKS, rows, 2 * cu), bf),
@@ -670,20 +719,21 @@
             collective_id=0, has_side_effects=True, vmem_limit_bytes=60 * 1024 * 1024
         ),
     )(
-        table,
-        sends,
+        mig_dest,
+        mig_from,
+        mig_to,
         kv_len,
         query,
         new_kv,
         resid,
-        norm_gain.reshape(1, -1),
+        norm_gain,
         kv_pool,
         w_out,
         w_gate,
         w_up,
         w_down,
     )
-    return result.reshape(steps, reqs, width)
+    return result
 
 
 def solution(mesh):

time: 107 us -> 93.6 us (0.87); the launches traced: 106 us -> 93.5 us
  Pallas kernels: 98 us -> 91.9 us
  other arithmetic: 4.78 us -> 0 us
  local copies, waits for them, and re-layouts: 2.84 us -> 1.55 us
    pallas_call x1, Pallas kernels: 98 us -> 91.9 us  [fused_body(): pl.pallas_call(layer_kernel, out_shape=jax.ShapeDtypeStruct((steps, reqs,...]
    reduce_sum x2 -> x0, other arithmetic: 1.46 us -> none  [the longest x1 1.28 us: fused_body(): jnp.sum(jnp.where(picked, mig_from[None, :], 0), axis=1).astype(jnp.int32)]
    add x2 -> x0, other arithmetic: 1.32 us -> none  [the longest x1 0.66 us: fused_body(): mig_dest * CAP + rank]
    reshape x1 -> x0, local copies, waits for them, and re-layouts: 1.28 us -> none  [fused_body(): norm_gain.reshape(1, -1)]
where the time goes in v2:
time: 93.6 us; the launch traced here: 93.5 us
  Pallas kernels  91.9 us (98%)
  local copies, waits for them, and re-layouts  1.55 us (2%)
    pallas_call x1, Pallas kernels, fused_body(): pl.pallas_call(layer_kernel, out_shape=jax.ShapeDtypeStruct((steps, reqs,...  91.9 us

profile of v2, /device:TPU:1, one launch (start us, length us, event | category | flops | bytes accessed | tf_op | source)
XLA Modules:
  0.0 93.5 jit_solution(7520328799212601197)
XLA Ops:
  0.0 91.9 %shard_map.127 = bf16[4,8,1792]{2,1,0:T(8,128)(2,1)} custom-call(s32[16]{0:T(128)} %mig_dest.1, s32[16]{0:T(128)} %mig_from.1, s32[16]{0:T(128)} %mig_to.1, s32[8]{0:T(128)} %lengths.1, bf16[4,8,4096]{2,1,0:T(8,128)(2,1)} %query.1, bf16[4,8,512]{2,1,0:T(8,128)(2,1)} %new_kv.1, bf16[4,32,1792]{2,1,0:T(8,128)(2,1)} %resid.1, bf16[1792]{0:T(1024)(128)(2,1)} %gain.1, ...), custom_call_target="tpu_custom_call" | custom-call | tf_op jit(solution)/shard_map/pallas_call | solution.py:682
  91.9 1.6 %copy.15 = bf16[4,8,1792]{2,1,0:T(8,128)(2,1)} copy(bf16[4,8,1792]{2,1,0:T(8,128)(2,1)} %shard_map.127) | data formatting | bytes 229376
